TPU v7x, 1024 devices: a whole 8x8x8 slice. The times are simulated.
1024 devices in a mesh: dp: 16 (over x, core), expert: 8 (over y), tensor: 8 (over z).
Axes of the slice: x: 8, y: 8, z: 8, core: 2. Of those that a mesh axis runs over, the one named last changes fastest.
Arguments:
- routes: int32 [8192, 2], P(('expert', 'tensor')), may hold values from 0 to 63, all different within a row; in each aligned block of 128 rows (0 to 127, 128 to 255, ...) at most 6 rows name the same one
- gate_scores: float32 [8192, 2], P(('expert', 'tensor')), may hold values from 0.1 to 1
- back_hidden: bfloat16 [64, 2432, 384], P(('expert', 'tensor'), 'dp'), may hold values from -6 to 6
- saved_gate: bfloat16 [64, 2432, 384], P(('expert', 'tensor'), 'dp'), may hold values from -6 to 6
- saved_up: bfloat16 [64, 2432, 384], P(('expert', 'tensor'), 'dp'), may hold values from -6 to 6
- expert_gate_w: bfloat16 [64, 2432, 3584], P(('expert', 'tensor'), 'dp'), may hold values from -0.09375 to 0.09375
- expert_up_w: bfloat16 [64, 2432, 3584], P(('expert', 'tensor'), 'dp'), may hold values from -0.09375 to 0.09375
- inputs_b: bfloat16 [3584, 32768], P('dp', ('expert', 'tensor')), may hold values from -6 to 6
- dense_gate_w: bfloat16 [2432, 3584], P('dp'), may hold values from -0.09375 to 0.09375
- dense_up_w: bfloat16 [2432, 3584], P('dp'), may hold values from -0.09375 to 0.09375
- dense_down_w: bfloat16 [2432, 3584], P('dp'), may hold values from -0.125 to 0.125
Outputs:
- grad_in_a: bfloat16 [3584, 8192], P('dp', ('expert', 'tensor'))
- dense_out_b: bfloat16 [3584, 32768], P('dp', ('expert', 'tensor'))
Inputs may be any that keep to these rules, and one draw needn't show every extreme that they name: `routes`: the two experts of a token differ. Among the 128 tokens of one group no expert is named more than 6 times, a bound that some block reaches in every draw.
All inputs are finite; a program needn't handle non-finite values.
Results may differ from a plain program's by a relative error of at most 0.024.
Values may be sent and summed in bfloat16 or wider, within the bound.
A program may use at most 64 MiB of HBM per device.

v0:
```python
import jax
import jax.numpy as jnp
from jax import lax
from jax.sharding import PartitionSpec as P


def slot_columns(routes, groups, capacity):
    flattened = routes.reshape(-1)
    onehot = (flattened[:, None] == jnp.arange(groups, dtype=jnp.int32)[None, :]).astype(jnp.int32)
    before = jnp.cumsum(onehot, axis=0) - onehot
    position = jnp.sum(before * onehot, axis=1)
    return (flattened * capacity + position).reshape(routes.shape)


def route_back(block):
    return lax.all_to_all(block, ("expert", "tensor"), split_axis=1, concat_axis=1, tiled=True)


def input_fold(weight_in, rows_piece):
    return jnp.dot(weight_in, rows_piece, preferred_element_type=jnp.float32)


def local(
    routes,
    gate_scores,
    back_hidden,
    saved_gate,
    saved_up,
    expert_gate_w,
    expert_up_w,
    inputs_b,
    dense_gate_w,
    dense_up_w,
    dense_down_w,
):
    groups = lax.axis_size(("expert", "tensor"))
    tokens_here = routes.shape[0]
    slot_count = 3 * tokens_here
    capacity = slot_count // groups
    columns = slot_columns(routes, groups, capacity)
    lane_ids = jnp.arange(slot_count, dtype=jnp.int32)
    weight_gate = expert_gate_w[0]
    weight_up = expert_up_w[0]
    back = back_hidden[0].astype(jnp.float32)
    gate_pre = saved_gate[0].astype(jnp.float32)
    up_pre = saved_up[0].astype(jnp.float32)
    sigmoid_g = jax.nn.sigmoid(gate_pre)
    grad_gate = (back * up_pre * sigmoid_g * (1.0 + gate_pre * (1.0 - sigmoid_g))).astype(
        jnp.bfloat16
    )
    grad_up = (back * gate_pre * sigmoid_g).astype(jnp.bfloat16)
    contract_first = (((0,), (0,)), ((), ()))
    rows_piece = lax.all_gather(inputs_b, "dp", axis=0, tiled=True)
    dense_gate = input_fold(dense_gate_w, rows_piece)
    dense_up = input_fold(dense_up_w, rows_piece)
    dense_hidden = (jax.nn.silu(dense_gate) * dense_up).astype(jnp.bfloat16)
    summed = lax.psum_scatter(
        jnp.concatenate(
            [
                lax.dot_general(
                    weight_gate, grad_gate, contract_first, preferred_element_type=jnp.float32
                )
                + lax.dot_general(
                    weight_up, grad_up, contract_first, preferred_element_type=jnp.float32
                ),
                lax.dot_general(
                    dense_down_w, dense_hidden, contract_first, preferred_element_type=jnp.float32
                ),
            ],
            axis=1,
        ).astype(jnp.bfloat16),
        "dp",
        scatter_dimension=0,
        tiled=True,
    ).astype(jnp.float32)
    returned = summed[:, :slot_count].astype(jnp.bfloat16)
    dense_out = summed[:, slot_count:].astype(jnp.bfloat16)
    arrived_back = route_back(returned)
    weighing = jnp.where(lane_ids[:, None] == columns[None, :, 0], gate_scores[None, :, 0], 0.0)
    weighing = weighing + jnp.where(
        lane_ids[:, None] == columns[None, :, 1], gate_scores[None, :, 1], 0.0
    )
    grad_in = jnp.dot(
        arrived_back.astype(jnp.float32),
        weighing,
        precision=lax.Precision.HIGHEST,
        preferred_element_type=jnp.float32,
    )
    return (grad_in.astype(jnp.bfloat16), dense_out)


def solution(mesh):
    in_specs = (
        P(("expert", "tensor"), None),
        P(("expert", "tensor"), None),
        P(("expert", "tensor"), "dp", None),
        P(("expert", "tensor"), "dp", None),
        P(("expert", "tensor"), "dp", None),
        P(("expert", "tensor"), "dp", None),
        P(("expert", "tensor"), "dp", None),
        P("dp", ("expert", "tensor")),
        P("dp", None),
        P("dp", None),
        P("dp", None),
    )
    out_specs = (P("dp", ("expert", "tensor")), P("dp", ("expert", "tensor")))
    return jax.shard_map(local, mesh=mesh, in_specs=in_specs, out_specs=out_specs, check_vma=False)
```

profile of v0, /device:TPU:7, one launch (start us, length us, event | category | flops | bytes accessed | tf_op | source)
XLA Modules:
  0.0 201.6 jit_solution(11287115413058619797)
XLA Ops:
  7.2 0.0 copy-start
  7.2 0.0 all-gather.2.cloned.1.call-start
  7.2 0.7 all-gather.2.cloned.1.call-update
  7.9 0.0 copy-start.1
  7.9 0.0 copy-start.3
  7.9 0.0 copy-start.4
  7.9 0.0 reduce-scatter.4.cloned.1.call-start
  8.0 2.4 %fusion.5 = f32[384,3584]{1,0:T(8,128)S(1)} fusion(bf16[1,152,3584]{2,1,0:T(8,128)(2,1)} %param.16, bf16[1,152,384]{2,1,0:T(8,128)(2,1)} %param.13, bf16[1,152,384]{2,1,0:T(8,128)(2,1)} %param.14, bf16[1,152,384]{2,1,0:T(8,128)(2,1)} %param.15), kind=kOutput, calls=%fused_computation.10 | convolution fusion | flops 419140608 | bytes 6944768 | tf_op jit(solution)/shard_map/dot_general | solution.py:60
  10.4 0.0 copy-done.1
  10.4 0.0 copy-done.3
  10.4 0.0 copy-done.4
  10.5 0.0 copy-start.2
  10.5 2.5 %fusion.2 = bf16[3584,384]{0,1:T(8,128)(2,1)} fusion(f32[384,3584]{1,0:T(8,128)S(1)} %fusion.5, bf16[1,152,3584]{2,1,0:T(8,128)(2,1)S(1)} %copy-done.1, bf16[1,152,384]{2,1,0:T(8,128)(2,1)S(1)} %copy-done.4, bf16[1,152,384]{2,1,0:T(8,128)(2,1)S(1)} %copy-done.3), kind=kOutput, calls=%fused_computation.5 | convolution fusion | flops 421601280 | bytes 9580544 | tf_op jit(solution)/shard_map/dot_general | solution.py:63
  13.0 55.8 %all-gather.2.cloned.1.call-done = bf16[3584,512]{1,0:T(8,128)(2,1)} async-done(((bf16[224,512]{1,0:T(8,128)(2,1)}), bf16[3584,512]{1,0:T(8,128)(2,1)}) %all-gather.2.cloned.1.call-update) | async-done | bytes 3670032 | tf_op jit(solution)/shard_map/all_gather | solution.py:53
  68.7 0.0 copy-done.2
  68.7 2.8 %fusion.42 = f32[152,512]{1,0:T(8,128)S(1)} fusion(bf16[152,3584]{1,0:T(8,128)(2,1)S(1)} %copy-done.2, bf16[3584,512]{1,0:T(8,128)(2,1)} %all-gather.2.cloned.1.call-done), kind=kOutput, calls=%fused_computation.61 | convolution fusion | flops 557842432 | bytes 5070848 | tf_op jit(solution)/shard_map/dot_general | solution.py:20
  71.5 0.0 copy-done
  71.5 6.2 %fusion.1 = bf16[3584,512]{0,1:T(8,128)(2,1)} fusion(bf16[152,3584]{1,0:T(8,128)(2,1)S(1)} %copy-done, bf16[152,3584]{1,0:T(8,128)(2,1)} %param.20, bf16[3584,512]{1,0:T(8,128)(2,1)} %all-gather.2.cloned.1.call-done, f32[152,512]{1,0:T(8,128)S(1)} %fusion.42), kind=kOutput, calls=%fused_computation.4 | convolution fusion | flops 1117986816 | bytes 9830400 | tf_op jit(solution)/shard_map/dot_general | solution.py:66
  77.7 6.0 %pad_maximum_fusion = bf16[3584,896]{0,1:T(8,128)(2,1)} fusion(bf16[3584,512]{0,1:T(8,128)(2,1)} %fusion.1, bf16[3584,384]{0,1:T(8,128)(2,1)} %fusion.2), kind=kLoop, calls=%fused_computation | loop fusion | flops 12845056 | bytes 12845056 | tf_op jit(solution)/shard_map/concatenate | solution.py:58
  83.7 9.6 %copy.37 = bf16[3584,896]{1,0:T(8,128)(2,1)} copy(bf16[3584,896]{0,1:T(8,128)(2,1)} %pad_maximum_fusion) | data formatting | bytes 12845056
  93.3 0.0 copy-start.5
  93.3 0.0 copy-start.6
  93.3 0.0 reduce-scatter.4.cloned.1.call-update
  93.3 0.7 copy-done.5
  93.9 0.1 copy.32
  94.1 0.1 eq.56
  94.2 0.1 eq.60
  94.4 0.6 reduce-window.6
  95.0 0.2 slice_reduce_fusion
  95.2 0.1 fusion.36
  95.3 0.1 reduce_sum.12
  95.5 0.1 copy.35
  95.5 69.5 %reduce-scatter.4.cloned.1.call-done = bf16[224,896]{1,0:T(8,128)(2,1)} async-done(((bf16[3584,896]{1,0:T(8,128)(2,1)}), bf16[224,896]{1,0:T(8,128)(2,1)}) %reduce-scatter.4.cloned.1.call-update) | async-done | bytes 401424
  165.1 0.9 slice.34
  166.0 0.1 copy.39
  166.2 0.8 all_to_all.8
  166.9 13.8 %all-to-all-start = ((bf16[224,64,6]{0,2,1:T(8,128)(2,1)}), bf16[224,64,6]{0,2,1:T(8,128)(2,1)S(1)}, u32[]{:S(2)}, u32[]{:S(2)}) async-start(bf16[224,64,6]{0,2,1:T(8,128)(2,1)} %all_to_all.8), calls=%async_computation | async-start | bytes 524288 | tf_op jit(solution)/shard_map/all_to_all | solution.py:16
  180.7 0.0 copy-done.6
  180.8 1.6 slice.36
  182.4 11.3 %all-to-all-done = bf16[224,64,6]{0,2,1:T(8,128)(2,1)S(1)} async-done(((bf16[224,64,6]{0,2,1:T(8,128)(2,1)}), bf16[224,64,6]{0,2,1:T(8,128)(2,1)S(1)}, u32[]{:S(2)}, u32[]{:S(2)}) %all-to-all-start) | async-done | bytes 172064 | tf_op jit(solution)/shard_map/all_to_all | solution.py:16
  193.7 0.1 all_to_all.10
  193.8 1.0 convolution_convert_fusion.1
  (6 shorter events, 0.1 us)
Async XLA Ops:
  7.2 64.4 %copy-start = (bf16[152,3584]{1,0:T(8,128)(2,1)S(1)}, bf16[152,3584]{1,0:T(8,128)(2,1)}, u32[]{:S(2)}) copy-start(bf16[152,3584]{1,0:T(8,128)(2,1)} %param.21) | copy-start | bytes 3268612
  7.2 61.6 %all-gather.2.cloned.1.call-start = ((), (), s32[]{:S(2)}) async-start(), calls=%async_computation.2 | async-start | bytes 3899392 | tf_op jit(solution)/shard_map/all_gather | solution.py:53
  7.9 2.5 %copy-start.1 = (bf16[1,152,3584]{2,1,0:T(8,128)(2,1)S(1)}, bf16[1,152,3584]{2,1,0:T(8,128)(2,1)}, u32[]{:S(2)}) copy-start(bf16[1,152,3584]{2,1,0:T(8,128)(2,1)} %param.17) | copy-start | bytes 3268612
  7.9 2.5 %copy-start.3 = (bf16[1,152,384]{2,1,0:T(8,128)(2,1)S(1)}, bf16[1,152,384]{2,1,0:T(8,128)(2,1)}, u32[]{:S(2)}) copy-start(bf16[1,152,384]{2,1,0:T(8,128)(2,1)} %param.13) | copy-start | bytes 350212
  7.9 2.5 %copy-start.4 = (bf16[1,152,384]{2,1,0:T(8,128)(2,1)S(1)}, bf16[1,152,384]{2,1,0:T(8,128)(2,1)}, u32[]{:S(2)}) copy-start(bf16[1,152,384]{2,1,0:T(8,128)(2,1)} %param.14) | copy-start | bytes 350212
  7.9 157.1 %reduce-scatter.4.cloned.1.call-start = ((), (), s32[]{:S(2)}) async-start(), calls=%async_computation.3 | async-start | bytes 6823936
  10.5 58.3 %copy-start.2 = (bf16[152,3584]{1,0:T(8,128)(2,1)S(1)}, bf16[152,3584]{1,0:T(8,128)(2,1)}, u32[]{:S(2)}) copy-start(bf16[152,3584]{1,0:T(8,128)(2,1)} %param.19) | copy-start | bytes 3268612
  93.3 0.7 copy-start.5
  93.3 87.5 %copy-start.6 = (f32[128,2]{0,1:T(2,128)S(1)}, f32[128,2]{0,1:T(2,128)}, u32[]{:S(2)}) copy-start(f32[128,2]{0,1:T(2,128)} %param.12) | copy-start | bytes 3076
  166.9 26.7 %all-to-all-start = ((bf16[224,64,6]{0,2,1:T(8,128)(2,1)}), bf16[224,64,6]{0,2,1:T(8,128)(2,1)S(1)}, u32[]{:S(2)}, u32[]{:S(2)}) async-start(bf16[224,64,6]{0,2,1:T(8,128)(2,1)} %all_to_all.8), calls=%async_computation | async-start | bytes 524288 | tf_op jit(solution)/shard_map/all_to_all | solution.py:16
Sparse Core Ops, SparseCore 0:
  10.7 57.9 all-gather.1
  93.4 71.6 reduce-scatter.3
where the time goes:
time: 202 us
  waiting for transfers between devices  137 us (68%)
  matrix products  14.9 us (7%)
  local copies, waits for them, and re-layouts  14.7 us (7%)
  between operations  14.2 us (7%)
  starting transfers between devices  13.8 us (7%)
  other arithmetic  6.78 us (3%)
    unnamed x3, waiting for transfers between devices  70.2 us
    all_gather x1, waiting for transfers between devices, local(): rows_piece = lax.all_gather(inputs_b, 'dp', axis=0, tiled=True)  55.8 us
    all_to_all x1, starting transfers between devices, route_back(): lax.all_to_all(block, ('expert', 'tensor'), split_axis=1, concat_axis=1,...  13.8 us
    all_to_all x1, waiting for transfers between devices, route_back(): lax.all_to_all(block, ('expert', 'tensor'), split_axis=1, concat_axis=1,...  11.3 us
    unnamed x17, local copies, waits for them, and re-layouts  10.5 us
    dot_general x1, matrix products, local(): lax.dot_general(dense_down_w, dense_hidden, contract_first, preferred_ele...  6.15 us
    concatenate x1, other arithmetic, local(): jnp.concatenate([lax.dot_general(weight_gate, grad_gate, contract_first,...  6.01 us
  transfers between devices with their start and end apart: 3, of which 3 were waited for; matrix products, arithmetic and copies ran while one was open for 4% of the time, Pallas kernels for 0%

commit v1 on v0

v1 whole, which is shorter than its diff:
```python
import functools

import jax
import jax.numpy as jnp
from jax import lax
from jax.experimental import pallas as pl
from jax.experimental.pallas import tpu as pltpu
from jax.sharding import PartitionSpec as P

MESH = pl.DeviceIdType.MESH
BF = jnp.bfloat16
F32 = jnp.float32
TN = (((0,), (0,)), ((), ()))
NT = (((1,), (1,)), ((), ()))


def kernel(
    nx, ny, nz, cap,
    routes_h, scores_h, back_h, sgate_h, sup_h, egw_h, euw_h, inb_h, dgw_h, duw_h, ddw_h,
    grad_o, dense_o,
    routes_v, scores_v, back_v, sgate_v, sup_v, egw_v, euw_v, dgw_v, duw_v, ddw_v,
    x_all, pe, qe, pd, qd, se, re, sd, rd,
    gg_v, gu_v, hid_v, ef_v, a1, a2, a3, a4, whi, wlo, perm,
    load_sem, ag_s, ag_r, sib_s, sib_r, qe_s, qe_r, qd_s, qd_r, se_s, re_s, sd_s, rd_s, y_s, y_r, z_s, z_r,
):
    feat = inb_h.shape[0]
    half = feat // 2
    slots = back_h.shape[2]
    toks = inb_h.shape[1]
    pair = 4 * feat
    npair = nx // 2
    far = nx // 2
    me = lax.axis_index("dp")
    x, c = me // 2, me % 2
    y, z = lax.axis_index("expert"), lax.axis_index("tensor")
    sib = x * 2 + 1 - c

    def chip(offset):
        return (x + offset + nx) % nx

    def dp_of(offset):
        return chip(offset) * 2 + c

    def rdma(src, dst, ssem, rsem, **where):
        return pltpu.make_async_remote_copy(
            src_ref=src, dst_ref=dst, send_sem=ssem, recv_sem=rsem, device_id=where, device_id_type=MESH
        )

    def rows(start, size):
        return pl.ds(pl.multiple_of(start, 16), size)

    loads = []
    sources = (sgate_h.at[0], back_h.at[0], sup_h.at[0], egw_h.at[0], euw_h.at[0], routes_h, scores_h, dgw_h, duw_h, ddw_h)
    targets = (sgate_v, back_v, sup_v, egw_v, euw_v, routes_v, scores_v, dgw_v, duw_v, ddw_v)
    for i, (src, dst) in enumerate(zip(sources, targets)):
        loads.append(pltpu.make_async_copy(src, dst, load_sem.at[i]))
    own_x = pltpu.make_async_copy(inb_h, x_all.at[rows(me * feat, feat), :], load_sem.at[len(sources)])
    own_x.start()
    for load in loads:
        load.start()

    barrier = pltpu.get_barrier_semaphore()
    partners = [dict(dp=dp_of(1)), dict(dp=dp_of(-1)), dict(dp=sib)]
    partners += [dict(expert=(y + k) % ny) for k in range(1, ny)]
    partners += [dict(tensor=(z + k) % nz) for k in range(1, nz)]
    for partner in partners:
        pl.semaphore_signal(barrier, inc=1, device_id=partner, device_id_type=MESH)
    pl.semaphore_wait(barrier, len(partners))

    pending = []

    def go(copy):
        copy.start()
        pending.append(copy)

    def x_rows(dp, h):
        return x_all.at[rows(dp * feat + h * half, half), :]

    def ag_send(d, hop, h):
        sign = 1 - 2 * d
        origin = dp_of(-sign * (hop - 1))
        src = inb_h.at[pl.ds(h * half, half), :] if hop == 1 else x_rows(origin, h)
        go(rdma(src, x_rows(origin, h), ag_s.at[d, hop - 1, h], ag_r.at[d, hop - 1, h], dp=dp_of(sign)))

    def ag_recv(d, hop, h):
        sign = 1 - 2 * d
        origin = dp_of(-sign * hop)
        ref = x_rows(origin, h)
        rdma(ref, ref, ag_s.at[d, hop - 1, h], ag_r.at[d, hop - 1, h], dp=dp_of(sign)).wait_recv()
        return origin

    def sib_send(slot, src, origin, h):
        go(rdma(src, x_rows(origin, h), sib_s.at[slot], sib_r.at[slot], dp=sib))

    def sib_recv(slot, offset, h):
        ref = x_rows(chip(offset) * 2 + 1 - c, h)
        rdma(ref, ref, sib_s.at[slot], sib_r.at[slot], dp=sib).wait_recv()

    def ag_pieces(hop):
        pieces = [(d, h) for h in range(2) for d in range(2)]
        if hop == far:
            pieces = [(d, h) for d, h in pieces if d == h]
        return pieces

    def ag_step(hop):
        for d, h in ag_pieces(hop):
            origin = ag_recv(d, hop, h)
            if hop < far and (hop + 1 < far or d == h):
                ag_send(d, hop + 1, h)
            sib_send(2 + (hop - 1) * 4 + d * 2 + h, x_rows(origin, h), origin, h)

    for d, h in ag_pieces(1):
        ag_send(d, 1, h)
    for h in range(2):
        sib_send(h, inb_h.at[pl.ds(h * half, half), :], me, h)

    for i in range(3):
        loads[i].wait()
    gate_pre = sgate_v[...].astype(F32)
    back = back_v[...].astype(F32)
    sig = jax.nn.sigmoid(gate_pre)
    gg_v[...] = (back * sup_v[...].astype(F32) * sig * (1.0 + gate_pre * (1.0 - sig))).astype(BF)
    gu_v[...] = (back * gate_pre * sig).astype(BF)
    loads[3].wait()
    loads[4].wait()

    pair_order = [npair // 2] + [k for k in range(npair) if k not in (0, npair // 2)] + [0]

    def chip_pair(j):
        return (x // 2 + pair_order[j]) % npair

    def expert_pair(j):
        p = chip_pair(j)
        lanes = pl.ds(pl.multiple_of(p * pair, 128), pair)
        out = lax.dot_general(egw_v[:, lanes], gg_v[...], TN, preferred_element_type=F32)
        out = out + lax.dot_general(euw_v[:, lanes], gu_v[...], TN, preferred_element_type=F32)
        pe[rows(p * pair, pair), :] = out.astype(BF)
        for i in range(2):
            q_send(pe, qe, qe_s, qe_r, p * 2 + i, j * 2 + i)

    def q_rows(q, there):
        return q.at[rows(there * feat, feat), :]

    def q_send(p, q, ss, rs, there, slot):
        src = p.at[rows((there * 2 + 1 - c) * feat, feat), :]
        go(rdma(src, q_rows(q, there), ss.at[slot], rs.at[slot], dp=sib))

    def q_recv(q, ss, rs, j):
        for i in range(2):
            ref = q_rows(q, chip_pair(j) * 2 + i)
            rdma(ref, ref, ss.at[j * 2 + i], rs.at[j * 2 + i], dp=sib).wait_recv()

    def slot_of(hop, h):
        return 0 if hop == 0 else 1 + (hop - 1) * 2 + h

    def partial(p, q, there, h):
        own = p[rows((there * 2 + c) * feat + h * half, half), :].astype(F32)
        return own + q[rows(there * feat + h * half, half), :].astype(F32)

    def rs_copy(s, r, ss, rs, d, slot):
        return rdma(s.at[d, slot], r.at[d, slot], ss.at[d, slot], rs.at[d, slot], dp=dp_of(1 - 2 * d))

    def rs_send(flow, d, hop, h):
        p, q, s, r, ss, rs = flow
        slot = slot_of(hop, h)
        total = partial(p, q, chip((1 - 2 * d) * (far - hop)), h)
        if hop > 1 or (hop == 1 and h == d):
            before = slot_of(hop - 1, h)
            rs_copy(s, r, ss, rs, d, before).wait_recv()
            total = total + r[d, before].astype(F32)
        s[d, slot] = total.astype(BF)
        go(rs_copy(s, r, ss, rs, d, slot))

    def rs_open(flow):
        for d in range(2):
            rs_send(flow, d, 0, d)

    def rs_open_1(flow):
        for d in range(2):
            rs_send(flow, d, 1, 1 - d)

    def rs_step(flow, hop):
        for h in range(2):
            for d in range(2):
                if hop > 1 or h == d:
                    rs_send(flow, d, hop, h)

    def rs_final(flow, h):
        p, q, s, r, ss, rs = flow
        total = partial(p, q, x, h)
        for d in range(2):
            slot = slot_of(far - 1, h)
            rs_copy(s, r, ss, rs, d, slot).wait_recv()
            total = total + r[d, slot].astype(F32)
        return total.astype(BF)

    eflow = (pe, qe, se, re, se_s, re_s)
    dflow = (pd, qd, sd, rd, sd_s, rd_s)

    expert_pair(0)
    ag_step(1)
    expert_pair(1)
    expert_pair(2)
    ag_step(2)
    expert_pair(3)

    loads[5].wait()
    loads[6].wait()
    n_tok = routes_v.shape[0]
    lane = lax.broadcasted_iota(jnp.int32, (n_tok, n_tok), 1)
    row = lax.broadcasted_iota(jnp.int32, (n_tok, n_tok), 0)
    named = [routes_v[:, k:k + 1] for k in range(2)]
    hot = [jnp.where(lane == named[k], 1.0, 0.0).astype(F32) for k in range(2)]
    earlier = jnp.where(lane < row, 1.0, 0.0).astype(BF)
    count = jnp.dot(earlier, (hot[0] + hot[1]).astype(BF), preferred_element_type=F32)
    lane_s = lax.broadcasted_iota(jnp.int32, (n_tok, slots), 1).astype(F32)
    weighing = jnp.zeros((n_tok, slots), F32)
    for k in range(2):
        rank = jnp.sum(count * hot[k], axis=1, keepdims=True)
        place = ((named[k] % nz) * (ny * cap) + (named[k] // nz) * cap).astype(F32) + rank
        weighing = weighing + jnp.where(lane_s == place, scores_v[:, k:k + 1], 0.0)
    high = weighing.astype(BF)
    whi[...] = high
    wlo[...] = (weighing - high.astype(F32)).astype(BF)
    row_s = lax.broadcasted_iota(jnp.int32, (slots, slots), 0)
    lane_t = lax.broadcasted_iota(jnp.int32, (slots, slots), 1)
    i_s = lax.broadcasted_iota(jnp.int32, (slots, 1), 0)
    j_s = ((i_s % (ny * cap)) // cap) * (nz * cap) + (i_s // (ny * cap)) * cap + i_s % cap
    perm[...] = jnp.where(lane_t == j_s, 1.0, 0.0).astype(BF)

    ag_step(3)
    q_recv(qe, qe_s, qe_r, 0)
    rs_open(eflow)
    q_recv(qe, qe_s, qe_r, 1)
    q_recv(qe, qe_s, qe_r, 2)
    rs_open_1(eflow)
    ag_step(4)
    own_x.wait()
    for h in range(2):
        sib_recv(h, 0, h)
    for hop in range(1, far + 1):
        for d, h in ag_pieces(hop):
            sib_recv(2 + (hop - 1) * 4 + d * 2 + h, -(1 - 2 * d) * hop, h)

    for i in range(7, 10):
        loads[i].wait()
    rs_step(eflow, 1)
    gate = jnp.dot(dgw_v[...], x_all[...], preferred_element_type=F32)
    up = jnp.dot(duw_v[...], x_all[...], preferred_element_type=F32)
    hid_v[...] = (gate * jax.nn.sigmoid(gate) * up).astype(BF)
    rs_step(eflow, 2)

    def dense_pair(j):
        p = chip_pair(j)
        lanes = pl.ds(pl.multiple_of(p * pair, 128), pair)
        out = lax.dot_general(ddw_v[:, lanes], hid_v[...], TN, preferred_element_type=F32)
        pd[rows(p * pair, pair), :] = out.astype(BF)
        for i in range(2):
            q_send(pd, qd, qd_s, qd_r, p * 2 + i, j * 2 + i)

    dense_pair(0)
    dense_pair(1)
    q_recv(qd, qd_s, qd_r, 0)
    rs_open(dflow)
    dense_pair(2)
    q_recv(qe, qe_s, qe_r, 3)
    rs_step(eflow, 3)
    q_recv(qd, qd_s, qd_r, 1)
    q_recv(qd, qd_s, qd_r, 2)
    rs_open_1(dflow)
    dense_pair(3)
    rs_step(dflow, 1)

    ef_v[pl.ds(2 * half, ef_v.shape[0] - 2 * half), :] = jnp.zeros((ef_v.shape[0] - 2 * half, slots), BF)
    for h in range(2):
        ef_v[pl.ds(h * half, half), :] = rs_final(eflow, h)
    eye = jnp.where(lane_t == row_s, 1.0, 0.0).astype(BF)
    a1[...] = lax.dot_general(eye, ef_v[...], NT, preferred_element_type=F32).astype(BF)
    ny_rows, nz_rows = nz * cap, ny * cap

    def y_copy(k):
        return rdma(
            a1.at[rows((y + k) % ny * ny_rows, ny_rows), :], a2.at[rows(y * ny_rows, ny_rows), :],
            y_s.at[k], y_r.at[k], expert=(y + k) % ny,
        )

    def z_copy(k):
        return rdma(
            a3.at[rows((z + k) % nz * nz_rows, nz_rows), :], a4.at[rows(z * nz_rows, nz_rows), :],
            z_s.at[k], z_r.at[k], tensor=(z + k) % nz,
        )

    def y_wait(k):
        ref = a2.at[rows((y - k + ny) % ny * ny_rows, ny_rows), :]
        rdma(ref, ref, y_s.at[k], y_r.at[k], expert=(y + k) % ny).wait_recv()

    def z_wait(k):
        ref = a4.at[rows((z - k + nz) % nz * nz_rows, nz_rows), :]
        rdma(ref, ref, z_s.at[k], z_r.at[k], tensor=(z + k) % nz).wait_recv()

    for k in range(1, ny):
        go(y_copy(k))
    a2[rows(y * ny_rows, ny_rows), :] = a1[rows(y * ny_rows, ny_rows), :]
    rs_step(dflow, 2)
    for k in range(1, ny):
        y_wait(k)
    a3[...] = jnp.dot(perm[...], a2[...], preferred_element_type=F32).astype(BF)
    for k in range(1, nz):
        go(z_copy(k))
    a4[rows(z * nz_rows, nz_rows), :] = a3[rows(z * nz_rows, nz_rows), :]
    q_recv(qd, qd_s, qd_r, 3)
    rs_step(dflow, 3)
    for k in range(1, nz):
        z_wait(k)
    mixed = jnp.dot(whi[...], a4[...], preferred_element_type=F32)
    mixed = mixed + jnp.dot(wlo[...], a4[...], preferred_element_type=F32)
    grad_o[...] = mixed.T[:feat, :].astype(BF)
    for h in range(2):
        dense_o[pl.ds(h * half, half), :] = rs_final(dflow, h)
    for copy in pending:
        copy.wait_send()


def local(ny, nz, routes, gate_scores, back_hidden, saved_gate, saved_up, egw, euw, inputs_b, dgw, duw, ddw):
    feat, toks = inputs_b.shape
    hid, model = dgw.shape
    slots = back_hidden.shape[2]
    n_tok = routes.shape[0]
    nx = model // feat // 2
    far = nx // 2
    cap = slots // (ny * nz)
    half = feat // 2
    wide = -(-feat // 128) * 128
    steps = 2 * far - 1
    vm, dma = pltpu.VMEM, pltpu.SemaphoreType.DMA
    scratch = [
        vm((n_tok, 2), jnp.int32), vm((n_tok, 2), F32),
        vm((hid, slots), BF), vm((hid, slots), BF), vm((hid, slots), BF),
        vm((hid, model), BF), vm((hid, model), BF), vm((hid, model), BF), vm((hid, model), BF), vm((hid, model), BF),
        vm((model, toks), BF),
        vm((model, slots), BF), vm((model // 2, slots), BF), vm((model, toks), BF), vm((model // 2, toks), BF),
        vm((2, steps, half, slots), BF), vm((2, steps, half, slots), BF),
        vm((2, steps, half, toks), BF), vm((2, steps, half, toks), BF),
        vm((hid, slots), BF), vm((hid, slots), BF), vm((hid, toks), BF), vm((wide, slots), BF),
        vm((slots, wide), BF), vm((slots, wide), BF), vm((slots, wide), BF), vm((slots, wide), BF),
        vm((n_tok, slots), BF), vm((n_tok, slots), BF), vm((slots, slots), BF),
        dma((11,)),
        dma((2, far, 2)), dma((2, far, 2)), dma((2 + 4 * far,)), dma((2 + 4 * far,)),
        dma((nx,)), dma((nx,)), dma((nx,)), dma((nx,)),
        dma((2, steps)), dma((2, steps)), dma((2, steps)), dma((2, steps)),
        dma((ny,)), dma((ny,)), dma((nz,)), dma((nz,)),
    ]
    return pl.pallas_call(
        functools.partial(kernel, nx, ny, nz, cap),
        out_shape=(jax.ShapeDtypeStruct((feat, n_tok), BF), jax.ShapeDtypeStruct((feat, toks), BF)),
        in_specs=[pl.BlockSpec(memory_space=pl.ANY)] * 11,
        out_specs=(pl.BlockSpec(memory_space=pltpu.VMEM), pl.BlockSpec(memory_space=pltpu.VMEM)),
        scratch_shapes=scratch,
        compiler_params=pltpu.CompilerParams(
            collective_id=0, has_side_effects=True, vmem_limit_bytes=52 * 1024 * 1024
        ),
    )(routes, gate_scores, back_hidden, saved_gate, saved_up, egw, euw, inputs_b, dgw, duw, ddw)


def solution(mesh):
    both = ("expert", "tensor")
    in_specs = (
        P(both, None), P(both, None),
        P(both, "dp", None), P(both, "dp", None), P(both, "dp", None), P(both, "dp", None), P(both, "dp", None),
        P("dp", both), P("dp", None), P("dp", None), P("dp", None),
    )
    out_specs = (P("dp", both), P("dp", both))
    body = functools.partial(local, mesh.shape["expert"], mesh.shape["tensor"])
    return jax.shard_map(body, mesh=mesh, in_specs=in_specs, out_specs=out_specs, check_vma=False)
```

time: 202 us -> 85.8 us (0.42)
  the two profiles are of different devices: /device:TPU:7 before, /device:TPU:4 now
where the time goes in v1:
time: 85.8 us; the launch traced here: 85.5 us
  Pallas kernels  78.4 us (91%)
  local copies, waits for them, and re-layouts  6.51 us (8%)
    pallas_call x1, Pallas kernels, local(): pl.pallas_call(functools.partial(kernel, nx, ny, nz, cap), out_shape=(jax...  78.4 us
    unnamed x12, local copies, waits for them, and re-layouts  6.51 us

profile of v1, /device:TPU:4, one launch (start us, length us, event | category | flops | bytes accessed | tf_op | source)
XLA Modules:
  0.0 85.5 jit_solution(6854121780044955394)
XLA Ops:
  0.6 0.8 copy.13.routes_h
  1.4 0.8 copy.14.scores_h
  2.2 0.0 copy-start
  2.2 0.9 %copy-done = bf16[224,512]{1,0:T(8,128)(2,1)S(1)} copy-done((bf16[224,512]{1,0:T(8,128)(2,1)S(1)}, bf16[224,512]{1,0:T(8,128)(2,1)}, u32[]{:S(2)}) %copy-start) | copy-done | bytes 229400
  3.1 0.0 copy-start.1
  3.1 0.9 %copy-done.1 = bf16[1,152,384]{2,1,0:T(8,128)(2,1)S(1)} copy-done((bf16[1,152,384]{2,1,0:T(8,128)(2,1)S(1)}, bf16[1,152,384]{2,1,0:T(8,128)(2,1)}, u32[]{:S(2)}) %copy-start.1) | copy-done | bytes 116760
  4.0 0.0 copy-start.2
  4.0 0.9 %copy-done.2 = bf16[1,152,384]{2,1,0:T(8,128)(2,1)S(1)} copy-done((bf16[1,152,384]{2,1,0:T(8,128)(2,1)S(1)}, bf16[1,152,384]{2,1,0:T(8,128)(2,1)}, u32[]{:S(2)}) %copy-start.2) | copy-done | bytes 116760
  4.9 0.0 copy-start.3
  4.9 0.9 %copy-done.3 = bf16[1,152,384]{2,1,0:T(8,128)(2,1)S(1)} copy-done((bf16[1,152,384]{2,1,0:T(8,128)(2,1)S(1)}, bf16[1,152,384]{2,1,0:T(8,128)(2,1)}, u32[]{:S(2)}) %copy-start.3) | copy-done | bytes 116760
  5.8 78.4 %shard_map.122 = (bf16[224,128]{1,0:T(8,128)(2,1)S(1)}, bf16[224,512]{1,0:T(8,128)(2,1)S(1)}) custom-call(s32[128,2]{1,0:T(8,128)S(1)} %copy.13.routes_h, f32[128,2]{1,0:T(8,128)S(1)} %copy.14.scores_h, bf16[1,152,384]{2,1,0:T(8,128)(2,1)S(1)} %copy-done.1, bf16[1,152,384]{2,1,0:T(8,128)(2,1)S(1)} %copy-done.2, bf16[1,152,384]{2,1,0:T(8,128)(2,1)S(1)} %copy-done.3, ...), custom_call_target="tpu_custom_call" | custom-call | tf_op jit(solution)/shard_map/pallas_call | solution.py:353
  84.2 0.6 copy.17
  84.8 0.7 copy.18
Async XLA Ops:
  2.2 0.9 %copy-start = (bf16[224,512]{1,0:T(8,128)(2,1)S(1)}, bf16[224,512]{1,0:T(8,128)(2,1)}, u32[]{:S(2)}) copy-start(bf16[224,512]{1,0:T(8,128)(2,1)} %inb_h.1) | copy-start | bytes 688132
  3.1 0.9 %copy-start.1 = (bf16[1,152,384]{2,1,0:T(8,128)(2,1)S(1)}, bf16[1,152,384]{2,1,0:T(8,128)(2,1)}, u32[]{:S(2)}) copy-start(bf16[1,152,384]{2,1,0:T(8,128)(2,1)} %back_h.1) | copy-start | bytes 350212
  4.0 0.9 %copy-start.2 = (bf16[1,152,384]{2,1,0:T(8,128)(2,1)S(1)}, bf16[1,152,384]{2,1,0:T(8,128)(2,1)}, u32[]{:S(2)}) copy-start(bf16[1,152,384]{2,1,0:T(8,128)(2,1)} %sgate_h.1) | copy-start | bytes 350212
  4.9 0.9 %copy-start.3 = (bf16[1,152,384]{2,1,0:T(8,128)(2,1)S(1)}, bf16[1,152,384]{2,1,0:T(8,128)(2,1)}, u32[]{:S(2)}) copy-start(bf16[1,152,384]{2,1,0:T(8,128)(2,1)} %sup_h.1) | copy-start | bytes 350212

commit v2 on v1

v2 whole, which is shorter than its diff:
```python
import functools

import jax
import jax.numpy as jnp
from jax import lax
from jax.experimental import pallas as pl
from jax.experimental.pallas import tpu as pltpu
from jax.sharding import PartitionSpec as P

MESH = pl.DeviceIdType.MESH
BF = jnp.bfloat16
F32 = jnp.float32
TN = (((0,), (0,)), ((), ()))
NT = (((1,), (1,)), ((), ()))


def kernel(
    nx, ny, nz, cap,
    routes_h, scores_h, back_h, sgate_h, sup_h, egw_h, euw_h, inb_h, dgw_h, duw_h, ddw_h,
    grad_o, dense_o,
    routes_v, scores_v, back_v, sgate_v, sup_v, egw_v, euw_v, dgw_v, duw_v, ddw_v,
    x_all, pe, qe, pd, qd, se, re, sd, rd,
    gg_v, gu_v, ef_v, a1, a2, a3, a4, whi, wlo, perm,
    meet, load_sem, ag_s, ag_r, sib_s, sib_r, qe_s, qe_r, qd_s, qd_r, se_s, re_s, sd_s, rd_s, y_s, y_r, z_s, z_r,
):
    feat = inb_h.shape[0]
    half = feat // 2
    slots = back_h.shape[2]
    part = inb_h.shape[1] // 2
    pair = 4 * feat
    npair = nx // 2
    far = nx // 2
    me = lax.axis_index("dp")
    x, c = me // 2, me % 2
    y, z = lax.axis_index("expert"), lax.axis_index("tensor")
    sib = x * 2 + 1 - c

    def chip(offset):
        return (x + offset + nx) % nx

    def dp_of(offset):
        return chip(offset) * 2 + c

    def rdma(src, dst, ssem, rsem, **where):
        return pltpu.make_async_remote_copy(
            src_ref=src, dst_ref=dst, send_sem=ssem, recv_sem=rsem, device_id=where, device_id_type=MESH
        )

    def rows(start, size):
        return pl.ds(pl.multiple_of(start, 16), size)

    loads = []
    sources = (sgate_h.at[0], back_h.at[0], sup_h.at[0], egw_h.at[0], euw_h.at[0], routes_h, scores_h, dgw_h, duw_h, ddw_h)
    targets = (sgate_v, back_v, sup_v, egw_v, euw_v, routes_v, scores_v, dgw_v, duw_v, ddw_v)
    for i, (src, dst) in enumerate(zip(sources, targets)):
        loads.append(pltpu.make_async_copy(src, dst, load_sem.at[i]))
    own_x = pltpu.make_async_copy(inb_h, x_all.at[rows(me * feat, feat), :], load_sem.at[len(sources)])
    own_x.start()
    for load in loads:
        load.start()

    barrier = pltpu.get_barrier_semaphore()
    y_z = [dict(expert=(y + k) % ny) for k in range(1, ny)]
    y_z += [dict(tensor=(z + k) % nz) for k in range(1, nz)]

    def signal(sem, **where):
        pl.semaphore_signal(sem, inc=1, device_id=where, device_id_type=MESH)

    @pl.when(c == 0)
    def _():
        signal(barrier, dp=dp_of(1))
        signal(barrier, dp=dp_of(-1))
        pl.semaphore_wait(barrier, 3)
        signal(meet.at[0], dp=dp_of(1))
        signal(meet.at[0], dp=dp_of(-1))
        pl.semaphore_wait(meet.at[0], 2)
        signal(meet.at[1], dp=sib)

    @pl.when(c == 1)
    def _():
        signal(barrier, dp=sib)
        pl.semaphore_wait(meet.at[1], 1)
        for where in y_z:
            signal(barrier, **where)

    def meet_y_z():
        @pl.when(c == 1)
        def _():
            if y_z:
                pl.semaphore_wait(barrier, len(y_z))
            signal(meet.at[2], dp=sib)

        @pl.when(c == 0)
        def _():
            pl.semaphore_wait(meet.at[2], 1)

    pending = []

    def go(copy):
        copy.start()
        pending.append(copy)

    def x_part(dp, t, h, size):
        return x_all.at[rows(dp * feat + h * half, size), pl.ds(t * part, part)]

    def ag_copy(d, t, hop, h, origin):
        src = dst = x_part(origin, t, h, half)
        if hop == 1:
            src = inb_h.at[pl.ds(h * half, half), pl.ds(t * part, part)]
        return rdma(src, dst, ag_s.at[t, d, hop - 1, h], ag_r.at[t, d, hop - 1, h], dp=dp_of(1 - 2 * d))

    def sib_copy(t, slot, h, origin, size):
        src = dst = x_part(origin, t, h, size)
        if slot == 0:
            src = inb_h.at[:, pl.ds(t * part, part)]
        return rdma(src, dst, sib_s.at[t, slot], sib_r.at[t, slot], dp=sib)

    def ag_open(t):
        for h in range(2):
            for d in range(2):
                go(ag_copy(d, t, 1, h, me))
        go(sib_copy(t, 0, 0, me, feat))

    def ag_step(t, hop):
        for h in range(2):
            for d in range(2):
                if hop == far and h != d:
                    continue
                origin = dp_of(-(1 - 2 * d) * hop)
                ag_copy(d, t, hop, h, origin).wait_recv()
                if hop + 1 < far or (hop + 1 == far and h == d):
                    go(ag_copy(d, t, hop + 1, h, origin))
                go(sib_copy(t, 1 + (hop - 1) * 4 + d * 2 + h, h, origin, half))

    def sib_wait(t):
        sib_copy(t, 0, 0, sib, feat).wait_recv()
        for hop in range(1, far + 1):
            for h in range(2):
                for d in range(2):
                    if hop < far or h == d:
                        origin = chip(-(1 - 2 * d) * hop) * 2 + 1 - c
                        sib_copy(t, 1 + (hop - 1) * 4 + d * 2 + h, h, origin, half).wait_recv()

    for t in range(2):
        ag_open(t)

    for i in range(3):
        loads[i].wait()
    gate_pre = sgate_v[...].astype(F32)
    back = back_v[...].astype(F32)
    sig = jax.nn.sigmoid(gate_pre)
    gg_v[...] = (back * sup_v[...].astype(F32) * sig * (1.0 + gate_pre * (1.0 - sig))).astype(BF)
    gu_v[...] = (back * gate_pre * sig).astype(BF)
    loads[3].wait()
    loads[4].wait()

    pair_order = [npair // 2] + [k for k in range(npair) if k not in (0, npair // 2)] + [0]

    def chip_pair(j):
        return (x // 2 + pair_order[j]) % npair

    def expert_pair(j):
        p = chip_pair(j)
        lanes = pl.ds(pl.multiple_of(p * pair, 128), pair)
        out = lax.dot_general(egw_v[:, lanes], gg_v[...], TN, preferred_element_type=F32)
        out = out + lax.dot_general(euw_v[:, lanes], gu_v[...], TN, preferred_element_type=F32)
        pe[rows(p * pair, pair), :] = out.astype(BF)
        for i in range(2):
            q_send(pe, qe, qe_s, qe_r, p * 2 + i, j * 2 + i)

    def q_rows(q, there):
        return q.at[rows(there * feat, feat), :]

    def q_send(p, q, ss, rs, there, slot):
        src = p.at[rows((there * 2 + 1 - c) * feat, feat), :]
        go(rdma(src, q_rows(q, there), ss.at[slot], rs.at[slot], dp=sib))

    def q_recv(q, ss, rs, j):
        for i in range(2):
            ref = q_rows(q, chip_pair(j) * 2 + i)
            rdma(ref, ref, ss.at[j * 2 + i], rs.at[j * 2 + i], dp=sib).wait_recv()

    def slot_of(hop, h):
        return 0 if hop == 0 else 1 + (hop - 1) * 2 + h

    def partial(p, q, there, h):
        own = p[rows((there * 2 + c) * feat + h * half, half), :].astype(F32)
        return own + q[rows(there * feat + h * half, half), :].astype(F32)

    def rs_copy(s, r, ss, rs, d, slot):
        return rdma(s.at[d, slot], r.at[d, slot], ss.at[d, slot], rs.at[d, slot], dp=dp_of(1 - 2 * d))

    def rs_send(flow, d, hop, h):
        p, q, s, r, ss, rs = flow
        slot = slot_of(hop, h)
        total = partial(p, q, chip((1 - 2 * d) * (far - hop)), h)
        if hop > 1 or (hop == 1 and h == d):
            before = slot_of(hop - 1, h)
            rs_copy(s, r, ss, rs, d, before).wait_recv()
            total = total + r[d, before].astype(F32)
        s[d, slot] = total.astype(BF)
        go(rs_copy(s, r, ss, rs, d, slot))

    def rs_open(flow):
        for d in range(2):
            rs_send(flow, d, 0, d)

    def rs_open_1(flow):
        for d in range(2):
            rs_send(flow, d, 1, 1 - d)

    def rs_step(flow, hop, other):
        for d in range(2):
            rs_send(flow, d, hop, 1 - d if other else d)

    def rs_final(flow, h):
        p, q, s, r, ss, rs = flow
        total = partial(p, q, x, h)
        for d in range(2):
            slot = slot_of(far - 1, h)
            rs_copy(s, r, ss, rs, d, slot).wait_recv()
            total = total + r[d, slot].astype(F32)
        return total.astype(BF)

    eflow = (pe, qe, se, re, se_s, re_s)
    dflow = [tuple(ref.at[t] for ref in (pd, qd, sd, rd, sd_s, rd_s)) for t in range(2)]

    for j in range(npair):
        expert_pair(j)
    for t in range(2):
        ag_step(t, 1)
    q_recv(qe, qe_s, qe_r, 0)
    rs_open(eflow)
    for j in range(1, npair):
        q_recv(qe, qe_s, qe_r, j)
    rs_open_1(eflow)

    loads[5].wait()
    loads[6].wait()
    n_tok = routes_v.shape[1]
    lane = lax.broadcasted_iota(jnp.int32, (n_tok, n_tok), 1)
    row = lax.broadcasted_iota(jnp.int32, (n_tok, n_tok), 0)
    named = [routes_v[k:k + 1, :] for k in range(2)]
    hot = [jnp.where(row == named[k], 1.0, 0.0).astype(F32) for k in range(2)]
    earlier = jnp.where(row < lane, 1.0, 0.0).astype(BF)
    count = jnp.dot((hot[0] + hot[1]).astype(BF), earlier, preferred_element_type=F32)
    place_s = lax.broadcasted_iota(jnp.int32, (slots, n_tok), 0).astype(F32)
    weighing = jnp.zeros((slots, n_tok), F32)
    for k in range(2):
        rank = jnp.sum(count * hot[k], axis=0, keepdims=True)
        place = ((named[k] % nz) * (ny * cap) + (named[k] // nz) * cap).astype(F32) + rank
        weighing = weighing + jnp.where(place_s == place, scores_v[k:k + 1, :], 0.0)
    high = weighing.astype(BF)
    whi[...] = high
    wlo[...] = (weighing - high.astype(F32)).astype(BF)
    row_s = lax.broadcasted_iota(jnp.int32, (slots, slots), 0)
    lane_t = lax.broadcasted_iota(jnp.int32, (slots, slots), 1)
    i_s = lax.broadcasted_iota(jnp.int32, (slots, 1), 0)
    j_s = ((i_s % (ny * cap)) // cap) * (nz * cap) + (i_s // (ny * cap)) * cap + i_s % cap
    perm[...] = jnp.where(lane_t == j_s, 1.0, 0.0).astype(BF)

    for t in range(2):
        ag_step(t, 2)
    for t in range(2):
        ag_step(t, 3)
    rs_step(eflow, 1, False)
    ag_step(0, 4)
    rs_step(eflow, 2, True)

    def dense_part(t):
        sib_wait(t)
        block = x_all[:, t * part:(t + 1) * part]
        gate = jnp.dot(dgw_v[...], block, preferred_element_type=F32)
        up = jnp.dot(duw_v[...], block, preferred_element_type=F32)
        hidden = (gate * jax.nn.sigmoid(gate) * up).astype(BF)
        p_t, q_t, ss, rs = pd.at[t], qd.at[t], qd_s.at[t], qd_r.at[t]
        for j in range(npair):
            p = chip_pair(j)
            lanes = pl.ds(pl.multiple_of(p * pair, 128), pair)
            out = lax.dot_general(ddw_v[:, lanes], hidden, TN, preferred_element_type=F32)
            p_t[rows(p * pair, pair), :] = out.astype(BF)
            for i in range(2):
                q_send(p_t, q_t, ss, rs, p * 2 + i, j * 2 + i)

    def dense_recv(t, j):
        q_recv(qd.at[t], qd_s.at[t], qd_r.at[t], j)

    own_x.wait()
    for i in range(7, 10):
        loads[i].wait()
    dense_part(0)
    ag_step(1, 4)
    rs_step(eflow, 2, False)
    dense_recv(0, 0)
    rs_open(dflow[0])
    dense_recv(0, 1)
    dense_recv(0, 2)
    rs_open_1(dflow[0])
    rs_step(eflow, 3, True)
    dense_part(1)
    rs_step(eflow, 3, False)
    dense_recv(1, 0)
    rs_open(dflow[1])
    dense_recv(1, 1)
    dense_recv(1, 2)
    rs_open_1(dflow[1])
    rs_step(dflow[0], 1, False)

    ef_v[pl.ds(2 * half, ef_v.shape[0] - 2 * half), :] = jnp.zeros((ef_v.shape[0] - 2 * half, slots), BF)
    for h in range(2):
        ef_v[pl.ds(h * half, half), :] = rs_final(eflow, h)
    eye = jnp.where(lane_t == row_s, 1.0, 0.0).astype(BF)
    a1[...] = lax.dot_general(eye, ef_v[...], NT, preferred_element_type=F32).astype(BF)
    ny_rows, nz_rows = nz * cap, ny * cap

    def y_copy(k):
        return rdma(
            a1.at[rows((y + k) % ny * ny_rows, ny_rows), :], a2.at[rows(y * ny_rows, ny_rows), :],
            y_s.at[k], y_r.at[k], expert=(y + k) % ny,
        )

    def z_copy(k):
        return rdma(
            a3.at[rows((z + k) % nz * nz_rows, nz_rows), :], a4.at[rows(z * nz_rows, nz_rows), :],
            z_s.at[k], z_r.at[k], tensor=(z + k) % nz,
        )

    def y_wait(k):
        ref = a2.at[rows((y - k + ny) % ny * ny_rows, ny_rows), :]
        rdma(ref, ref, y_s.at[k], y_r.at[k], expert=(y + k) % ny).wait_recv()

    def z_wait(k):
        ref = a4.at[rows((z - k + nz) % nz * nz_rows, nz_rows), :]
        rdma(ref, ref, z_s.at[k], z_r.at[k], tensor=(z + k) % nz).wait_recv()

    meet_y_z()
    for k in range(1, ny):
        go(y_copy(k))
    a2[rows(y * ny_rows, ny_rows), :] = a1[rows(y * ny_rows, ny_rows), :]
    rs_step(dflow[1], 1, False)
    rs_step(dflow[0], 2, True)
    rs_step(dflow[0], 2, False)
    for k in range(1, ny):
        y_wait(k)
    a3[...] = jnp.dot(perm[...], a2[...], preferred_element_type=F32).astype(BF)
    for k in range(1, nz):
        go(z_copy(k))
    a4[rows(z * nz_rows, nz_rows), :] = a3[rows(z * nz_rows, nz_rows), :]
    rs_step(dflow[1], 2, True)
    rs_step(dflow[1], 2, False)
    dense_recv(0, 3)
    dense_recv(1, 3)
    rs_step(dflow[0], 3, True)
    rs_step(dflow[0], 3, False)
    rs_step(dflow[1], 3, True)
    rs_step(dflow[1], 3, False)
    for t in range(2):
        for h in range(2):
            dense_o[pl.ds(h * half, half), pl.ds(t * part, part)] = rs_final(dflow[t], h)
    for k in range(1, nz):
        z_wait(k)
    mixed = lax.dot_general(a4[...], whi[...], TN, preferred_element_type=F32)
    mixed = mixed + lax.dot_general(a4[...], wlo[...], TN, preferred_element_type=F32)
    grad_o[...] = mixed[:feat, :].astype(BF)
    for copy in pending:
        copy.wait_send()


def local(ny, nz, routes, gate_scores, back_hidden, saved_gate, saved_up, egw, euw, inputs_b, dgw, duw, ddw):
    feat, toks = inputs_b.shape
    hid, model = dgw.shape
    slots = back_hidden.shape[2]
    n_tok = routes.shape[0]
    nx = model // feat // 2
    far = nx // 2
    cap = slots // (ny * nz)
    half = feat // 2
    part = toks // 2
    wide = -(-feat // 128) * 128
    steps = 2 * far - 1
    vm, dma = pltpu.VMEM, pltpu.SemaphoreType.DMA
    scratch = [
        vm((2, n_tok), jnp.int32), vm((2, n_tok), F32),
        vm((hid, slots), BF), vm((hid, slots), BF), vm((hid, slots), BF),
        vm((hid, model), BF), vm((hid, model), BF), vm((hid, model), BF), vm((hid, model), BF), vm((hid, model), BF),
        vm((model, toks), BF),
        vm((model, slots), BF), vm((model // 2, slots), BF), vm((2, model, part), BF), vm((2, model // 2, part), BF),
        vm((2, steps, half, slots), BF), vm((2, steps, half, slots), BF),
        vm((2, 2, steps, half, part), BF), vm((2, 2, steps, half, part), BF),
        vm((hid, slots), BF), vm((hid, slots), BF), vm((wide, slots), BF),
        vm((slots, wide), BF), vm((slots, wide), BF), vm((slots, wide), BF), vm((slots, wide), BF),
        vm((slots, n_tok), BF), vm((slots, n_tok), BF), vm((slots, slots), BF),
        pltpu.SemaphoreType.REGULAR((3,)), dma((11,)),
        dma((2, 2, far, 2)), dma((2, 2, far, 2)), dma((2, 1 + 4 * far)), dma((2, 1 + 4 * far)),
        dma((nx,)), dma((nx,)), dma((2, nx)), dma((2, nx)),
        dma((2, steps)), dma((2, steps)), dma((2, 2, steps)), dma((2, 2, steps)),
        dma((ny,)), dma((ny,)), dma((nz,)), dma((nz,)),
    ]
    return pl.pallas_call(
        functools.partial(kernel, nx, ny, nz, cap),
        out_shape=(pltpu.VMEM((feat, n_tok), BF), pltpu.VMEM((feat, toks), BF)),
        in_specs=[pl.BlockSpec(memory_space=pltpu.HBM)] * 11,
        out_specs=(pl.BlockSpec(memory_space=pltpu.VMEM), pl.BlockSpec(memory_space=pltpu.VMEM)),
        scratch_shapes=scratch,
        compiler_params=pltpu.CompilerParams(
            collective_id=0, has_side_effects=True, vmem_limit_bytes=62 * 1024 * 1024
        ),
    )(routes.T, gate_scores.T, back_hidden, saved_gate, saved_up, egw, euw, inputs_b, dgw, duw, ddw)


def solution(mesh):
    both = ("expert", "tensor")
    in_specs = (
        P(both, None), P(both, None),
        P(both, "dp", None), P(both, "dp", None), P(both, "dp", None), P(both, "dp", None), P(both, "dp", None),
        P("dp", both), P("dp", None), P("dp", None), P("dp", None),
    )
    out_specs = (P("dp", both), P("dp", both))
    body = functools.partial(local, mesh.shape["expert"], mesh.shape["tensor"])
    return jax.shard_map(body, mesh=mesh, in_specs=in_specs, out_specs=out_specs, check_vma=False)
```

time: 85.8 us -> 77.5 us (0.903)
  the two profiles are of different devices: /device:TPU:4 before, /device:TPU:2 now
where the time goes in v2:
time: 77.5 us; the launch traced here: 77.4 us
  Pallas kernels  75.4 us (97%)
  local copies, waits for them, and re-layouts  1.31 us (2%)
    pallas_call x1, Pallas kernels, local(): pl.pallas_call(functools.partial(kernel, nx, ny, nz, cap), out_shape=(plt...  75.4 us

profile of v2, /device:TPU:2, one launch (start us, length us, event | category | flops | bytes accessed | tf_op | source)
XLA Modules:
  0.0 77.4 jit_solution(9137723260025458673)
XLA Ops:
  0.6 75.4 %shard_map.122 = (bf16[224,128]{1,0:T(8,128)(2,1)S(1)}, bf16[224,512]{1,0:T(8,128)(2,1)S(1)}) custom-call(s32[2,128]{1,0:T(2,128)} %bitcast.2, f32[2,128]{1,0:T(2,128)} %bitcast.3, bf16[1,152,384]{2,1,0:T(8,128)(2,1)} %back_h.1, bf16[1,152,384]{2,1,0:T(8,128)(2,1)} %sgate_h.1, bf16[1,152,384]{2,1,0:T(8,128)(2,1)} %sup_h.1, bf16[1,152,3584]{2,1,0:T(8,128)(2,1)} %egw_h.1, ...), custom_call_target="tpu_custom_call" | custom-call | tf_op jit(solution)/shard_map/pallas_call | solution.py:399
  76.1 0.6 copy.15
  76.7 0.7 copy.16

commit v3 on v2

--- a/solution.py
+++ b/solution.py
@@ -19,12 +19,14 @@
     routes_h, scores_h, back_h, sgate_h, sup_h, egw_h, euw_h, inb_h, dgw_h, duw_h, ddw_h,
     grad_o, dense_o,
     routes_v, scores_v, back_v, sgate_v, sup_v, egw_v, euw_v, dgw_v, duw_v, ddw_v,
-    x_all, pe, qe, pd, qd, se, re, sd, rd,
+    x_all, h_all, w_all, w_cut, pe, qe, se, re,
     gg_v, gu_v, ef_v, a1, a2, a3, a4, whi, wlo, perm,
-    meet, load_sem, ag_s, ag_r, sib_s, sib_r, qe_s, qe_r, qd_s, qd_r, se_s, re_s, sd_s, rd_s, y_s, y_r, z_s, z_r,
+    meet, load_sem, ag_s, ag_r, sib_s, sib_r, hg_s, hg_r, hsib_s, hsib_r, wx_s, wx_r, wz_s, wz_r, wy_s, wy_r,
+    qe_s, qe_r, se_s, re_s, y_s, y_r, z_s, z_r,
 ):
     feat = inb_h.shape[0]
     half = feat // 2
+    hid_rows = h_all.shape[0] // (2 * nx)
     slots = back_h.shape[2]
     part = inb_h.shape[1] // 2
     pair = 4 * feat
@@ -59,6 +61,55 @@
     for load in loads:
         load.start()
 
+    def gather(buf, size, own, ss, rs, sib_ss, sib_rs):
+        part_rows = size // 2
+
+        def piece(dp, t, h, n):
+            return buf.at[rows(dp * size + h * part_rows, n), pl.ds(t * part, part)]
+
+        def ring_copy(d, t, hop, h, origin):
+            src = dst = piece(origin, t, h, part_rows)
+            if hop == 1 and own is not None:
+                src = own.at[pl.ds(h * part_rows, part_rows), pl.ds(t * part, part)]
+            return rdma(src, dst, ss.at[t, d, hop - 1, h], rs.at[t, d, hop - 1, h], dp=dp_of(1 - 2 * d))
+
+        def sib_copy(t, slot, h, origin, n):
+            src = dst = piece(origin, t, h, n)
+            if slot == 0 and own is not None:
+                src = own.at[:, pl.ds(t * part, part)]
+            return rdma(src, dst, sib_ss.at[t, slot], sib_rs.at[t, slot], dp=sib)
+
+        def first(t):
+            return [ring_copy(d, t, 1, h, me) for h in range(2) for d in range(2)] + [sib_copy(t, 0, 0, me, size)]
+
+        def step(t, hop):
+            for h in range(2):
+                for d in range(2):
+                    if hop == far and h != d:
+                        continue
+                    origin = dp_of(-(1 - 2 * d) * hop)
+                    ring_copy(d, t, hop, h, origin).wait_recv()
+                    if hop + 1 < far or (hop + 1 == far and h == d):
+                        go(ring_copy(d, t, hop + 1, h, origin))
+                    go(sib_copy(t, 1 + (hop - 1) * 4 + d * 2 + h, h, origin, part_rows))
+
+        def finish(t):
+            sib_copy(t, 0, 0, sib, size).wait_recv()
+            for hop in range(1, far + 1):
+                for h in range(2):
+                    for d in range(2):
+                        if hop < far or h == d:
+                            origin = chip(-(1 - 2 * d) * hop) * 2 + 1 - c
+                            sib_copy(t, 1 + (hop - 1) * 4 + d * 2 + h, h, origin, part_rows).wait_recv()
+
+        return first, step, finish
+
+    x_first, x_step, x_finish = gather(x_all, feat, inb_h, ag_s, ag_r, sib_s, sib_r)
+    h_first, h_step, h_finish = gather(h_all, hid_rows, None, hg_s, hg_r, hsib_s, hsib_r)
+
+    def x_copies():
+        return x_first(0) + x_first(1)
+
     barrier = pltpu.get_barrier_semaphore()
     y_z = [dict(expert=(y + k) % ny) for k in range(1, ny)]
     y_z += [dict(tensor=(z + k) % nz) for k in range(1, nz)]
@@ -68,18 +119,22 @@
 
     @pl.when(c == 0)
     def _():
-        signal(barrier, dp=dp_of(1))
-        signal(barrier, dp=dp_of(-1))
-        pl.semaphore_wait(barrier, 3)
-        signal(meet.at[0], dp=dp_of(1))
-        signal(meet.at[0], dp=dp_of(-1))
-        pl.semaphore_wait(meet.at[0], 2)
+        for k in range(1, nx):
+            signal(barrier, dp=dp_of(k))
+        pl.semaphore_wait(barrier, nx)
+        for k in range(1, nx):
+            signal(meet.at[0], dp=dp_of(k))
+        for copy in x_copies():
+            copy.start()
+        pl.semaphore_wait(meet.at[0], nx - 1)
         signal(meet.at[1], dp=sib)
 
     @pl.when(c == 1)
     def _():
         signal(barrier, dp=sib)
         pl.semaphore_wait(meet.at[1], 1)
+        for copy in x_copies():
+            copy.start()
         for where in y_z:
             signal(barrier, **where)
 
@@ -100,49 +155,7 @@
         copy.start()
         pending.append(copy)
 
-    def x_part(dp, t, h, size):
-        return x_all.at[rows(dp * feat + h * half, size), pl.ds(t * part, part)]
-
-    def ag_copy(d, t, hop, h, origin):
-        src = dst = x_part(origin, t, h, half)
-        if hop == 1:
-            src = inb_h.at[pl.ds(h * half, half), pl.ds(t * part, part)]
-        return rdma(src, dst, ag_s.at[t, d, hop - 1, h], ag_r.at[t, d, hop - 1, h], dp=dp_of(1 - 2 * d))
-
-    def sib_copy(t, slot, h, origin, size):
-        src = dst = x_part(origin, t, h, size)
-        if slot == 0:
-            src = inb_h.at[:, pl.ds(t * part, part)]
-        return rdma(src, dst, sib_s.at[t, slot], sib_r.at[t, slot], dp=sib)
-
-    def ag_open(t):
-        for h in range(2):
-            for d in range(2):
-                go(ag_copy(d, t, 1, h, me))
-        go(sib_copy(t, 0, 0, me, feat))
-
-    def ag_step(t, hop):
-        for h in range(2):
-            for d in range(2):
-                if hop == far and h != d:
-                    continue
-                origin = dp_of(-(1 - 2 * d) * hop)
-                ag_copy(d, t, hop, h, origin).wait_recv()
-                if hop + 1 < far or (hop + 1 == far and h == d):
-                    go(ag_copy(d, t, hop + 1, h, origin))
-                go(sib_copy(t, 1 + (hop - 1) * 4 + d * 2 + h, h, origin, half))
-
-    def sib_wait(t):
-        sib_copy(t, 0, 0, sib, feat).wait_recv()
-        for hop in range(1, far + 1):
-            for h in range(2):
-                for d in range(2):
-                    if hop < far or h == d:
-                        origin = chip(-(1 - 2 * d) * hop) * 2 + 1 - c
-                        sib_copy(t, 1 + (hop - 1) * 4 + d * 2 + h, h, origin, half).wait_recv()
-
-    for t in range(2):
-        ag_open(t)
+    pending.extend(x_copies())
 
     for i in range(3):
         loads[i].wait()
@@ -223,17 +236,70 @@
         return total.astype(BF)
 
     eflow = (pe, qe, se, re, se_s, re_s)
-    dflow = [tuple(ref.at[t] for ref in (pd, qd, sd, rd, sd_s, rd_s)) for t in range(2)]
+
+    w_src = 2 * y + z // (nz // 2 or 1)
+    w_half = hid_rows // 2
+
+    def w_place(zz):
+        return zz // 2 % 2 * w_half, pl.ds(pl.multiple_of(zz % 2 * 128, 128), 128)
+
+    def w_part(zz):
+        low, lanes = w_place(zz)
+        return w_all.at[rows((2 * y + zz // (nz // 2 or 1)) * hid_rows + low, w_half), lanes]
+
+    def w_x_copy(k):
+        low, lanes = w_place(z)
+        there = (me + k) % (2 * nx)
+        return rdma(w_cut.at[there, rows(low, w_half), lanes], w_part(z), wx_s.at[k], wx_r.at[0], dp=there)
+
+    def w_cut_send():
+        loads[9].wait()
+
+        @pl.when(me == w_src)
+        def _():
+            w_cut[...] = jnp.zeros(w_cut.shape, BF)
+            for q in range(2 * nx):
+                w_cut[q, 0:ddw_v.shape[0], 0:feat] = ddw_v[:, q * feat:(q + 1) * feat]
+            for k in range(1, 2 * nx):
+                w_x_copy(k).start()
+            low, lanes = w_place(z)
+            mine = pltpu.make_async_copy(w_cut.at[me, rows(low, w_half), lanes], w_part(z), wx_s.at[0])
+            mine.start()
+            mine.wait()
+
+    def w_cut_recv():
+        @pl.when(me != w_src)
+        def _():
+            w_x_copy(1).wait_recv()
+
+    def w_z_copy(k, zz):
+        return rdma(w_part(zz), w_part(zz), wz_s.at[k], wz_r.at[k], tensor=(z + k) % nz)
+
+    def w_y_copy(d, hop, origin):
+        low, size = (origin * 2 * hid_rows, 2 * hid_rows) if hop < ny // 2 else ((origin * 2 + d) * hid_rows, hid_rows)
+        ref = w_all.at[rows(low, size), :]
+        return rdma(ref, ref, wy_s.at[d, hop - 1], wy_r.at[d, hop - 1], expert=(y + 1 - 2 * d + ny) % ny)
+
+    def w_y_step(hop):
+        if hop > ny // 2:
+            return
+        for d in range(2):
+            origin = (y - (1 - 2 * d) * hop + ny) % ny
+            w_y_copy(d, hop, origin).wait_recv()
+            if hop < ny // 2:
+                go(w_y_copy(d, hop + 1, origin))
 
     for j in range(npair):
         expert_pair(j)
-    for t in range(2):
-        ag_step(t, 1)
+    w_cut_send()
+    x_step(0, 1)
     q_recv(qe, qe_s, qe_r, 0)
     rs_open(eflow)
+    x_step(1, 1)
     for j in range(1, npair):
         q_recv(qe, qe_s, qe_r, j)
     rs_open_1(eflow)
+    x_step(0, 2)
 
     loads[5].wait()
     loads[6].wait()
@@ -259,52 +325,50 @@
     j_s = ((i_s % (ny * cap)) // cap) * (nz * cap) + (i_s // (ny * cap)) * cap + i_s % cap
     perm[...] = jnp.where(lane_t == j_s, 1.0, 0.0).astype(BF)
 
-    for t in range(2):
-        ag_step(t, 2)
-    for t in range(2):
-        ag_step(t, 3)
     rs_step(eflow, 1, False)
-    ag_step(0, 4)
+    x_step(1, 2)
     rs_step(eflow, 2, True)
-
-    def dense_part(t):
-        sib_wait(t)
+    x_step(0, 3)
+    rs_step(eflow, 2, False)
+    w_cut_recv()
+    meet_y_z()
+    for k in range(1, nz):
+        go(w_z_copy(k, z))
+    x_step(1, 3)
+    rs_step(eflow, 3, True)
+    x_step(0, 4)
+
+    def hidden_part(t):
+        x_finish(t)
         block = x_all[:, t * part:(t + 1) * part]
         gate = jnp.dot(dgw_v[...], block, preferred_element_type=F32)
         up = jnp.dot(duw_v[...], block, preferred_element_type=F32)
-        hidden = (gate * jax.nn.sigmoid(gate) * up).astype(BF)
-        p_t, q_t, ss, rs = pd.at[t], qd.at[t], qd_s.at[t], qd_r.at[t]
-        for j in range(npair):
-            p = chip_pair(j)
-            lanes = pl.ds(pl.multiple_of(p * pair, 128), pair)
-            out = lax.dot_general(ddw_v[:, lanes], hidden, TN, preferred_element_type=F32)
-            p_t[rows(p * pair, pair), :] = out.astype(BF)
-            for i in range(2):
-                q_send(p_t, q_t, ss, rs, p * 2 + i, j * 2 + i)
-
-    def dense_recv(t, j):
-        q_recv(qd.at[t], qd_s.at[t], qd_r.at[t], j)
+        hidden = gate * jax.nn.sigmoid(gate) * up
+        hidden = jnp.concatenate([hidden, jnp.zeros((hid_rows - hidden.shape[0], part), F32)], axis=0)
+        h_all[rows(me * hid_rows, hid_rows), t * part:(t + 1) * part] = hidden.astype(BF)
+        for copy in h_first(t):
+            go(copy)
+
+    def dense_part(t):
+        h_finish(t)
+        block = h_all[:, t * part:(t + 1) * part]
+        out = lax.dot_general(w_all[...], block, TN, preferred_element_type=F32)
+        dense_o[:, t * part:(t + 1) * part] = out[:feat, :].astype(BF)
 
     own_x.wait()
-    for i in range(7, 10):
+    for i in range(7, 9):
         loads[i].wait()
-    dense_part(0)
-    ag_step(1, 4)
-    rs_step(eflow, 2, False)
-    dense_recv(0, 0)
-    rs_open(dflow[0])
-    dense_recv(0, 1)
-    dense_recv(0, 2)
-    rs_open_1(dflow[0])
-    rs_step(eflow, 3, True)
-    dense_part(1)
+    hidden_part(0)
+    for k in range(1, nz):
+        w_z_copy(k, (z - k + nz) % nz).wait_recv()
+    if ny > 1:
+        for d in range(2):
+            go(w_y_copy(d, 1, y))
     rs_step(eflow, 3, False)
-    dense_recv(1, 0)
-    rs_open(dflow[1])
-    dense_recv(1, 1)
-    dense_recv(1, 2)
-    rs_open_1(dflow[1])
-    rs_step(dflow[0], 1, False)
+    x_step(1, 4)
+    hidden_part(1)
+    w_y_step(1)
+    h_step(0, 1)
 
     ef_v[pl.ds(2 * half, ef_v.shape[0] - 2 * half), :] = jnp.zeros((ef_v.shape[0] - 2 * half, slots), BF)
     for h in range(2):
@@ -333,35 +397,38 @@
         ref = a4.at[rows((z - k + nz) % nz * nz_rows, nz_rows), :]
         rdma(ref, ref, z_s.at[k], z_r.at[k], tensor=(z + k) % nz).wait_recv()
 
-    meet_y_z()
     for k in range(1, ny):
         go(y_copy(k))
     a2[rows(y * ny_rows, ny_rows), :] = a1[rows(y * ny_rows, ny_rows), :]
-    rs_step(dflow[1], 1, False)
-    rs_step(dflow[0], 2, True)
-    rs_step(dflow[0], 2, False)
+    h_step(1, 1)
+    w_y_step(2)
+    h_step(0, 2)
     for k in range(1, ny):
         y_wait(k)
     a3[...] = jnp.dot(perm[...], a2[...], preferred_element_type=F32).astype(BF)
     for k in range(1, nz):
         go(z_copy(k))
     a4[rows(z * nz_rows, nz_rows), :] = a3[rows(z * nz_rows, nz_rows), :]
-    rs_step(dflow[1], 2, True)
-    rs_step(dflow[1], 2, False)
-    dense_recv(0, 3)
-    dense_recv(1, 3)
-    rs_step(dflow[0], 3, True)
-    rs_step(dflow[0], 3, False)
-    rs_step(dflow[1], 3, True)
-    rs_step(dflow[1], 3, False)
+    h_step(1, 2)
+    w_y_step(3)
+    h_step(0, 3)
+    h_step(1, 3)
+    w_y_step(4)
+    h_step(0, 4)
+    h_step(1, 4)
     for t in range(2):
-        for h in range(2):
-            dense_o[pl.ds(h * half, half), pl.ds(t * part, part)] = rs_final(dflow[t], h)
+        dense_part(t)
     for k in range(1, nz):
         z_wait(k)
     mixed = lax.dot_general(a4[...], whi[...], TN, preferred_element_type=F32)
     mixed = mixed + lax.dot_general(a4[...], wlo[...], TN, preferred_element_type=F32)
     grad_o[...] = mixed[:feat, :].astype(BF)
+
+    @pl.when(me == w_src)
+    def _():
+        for k in range(1, 2 * nx):
+            w_x_copy(k).wait_send()
+
     for copy in pending:
         copy.wait_send()
 
@@ -376,6 +443,7 @@
     cap = slots // (ny * nz)
     half = feat // 2
     part = toks // 2
+    hid_rows = -(-hid // 32) * 32
     wide = -(-feat // 128) * 128
     steps = 2 * far - 1
     vm, dma = pltpu.VMEM, pltpu.SemaphoreType.DMA
@@ -383,17 +451,18 @@
         vm((2, n_tok), jnp.int32), vm((2, n_tok), F32),
         vm((hid, slots), BF), vm((hid, slots), BF), vm((hid, slots), BF),
         vm((hid, model), BF), vm((hid, model), BF), vm((hid, model), BF), vm((hid, model), BF), vm((hid, model), BF),
-        vm((model, toks), BF),
-        vm((model, slots), BF), vm((model // 2, slots), BF), vm((2, model, part), BF), vm((2, model // 2, part), BF),
+        vm((model, toks), BF), vm((2 * nx * hid_rows, toks), BF), vm((2 * nx * hid_rows, wide), BF), vm((2 * nx, hid_rows, wide), BF),
+        vm((model, slots), BF), vm((model // 2, slots), BF),
         vm((2, steps, half, slots), BF), vm((2, steps, half, slots), BF),
-        vm((2, 2, steps, half, part), BF), vm((2, 2, steps, half, part), BF),
         vm((hid, slots), BF), vm((hid, slots), BF), vm((wide, slots), BF),
         vm((slots, wide), BF), vm((slots, wide), BF), vm((slots, wide), BF), vm((slots, wide), BF),
         vm((slots, n_tok), BF), vm((slots, n_tok), BF), vm((slots, slots), BF),
         pltpu.SemaphoreType.REGULAR((3,)), dma((11,)),
         dma((2, 2, far, 2)), dma((2, 2, far, 2)), dma((2, 1 + 4 * far)), dma((2, 1 + 4 * far)),
-        dma((nx,)), dma((nx,)), dma((2, nx)), dma((2, nx)),
-        dma((2, steps)), dma((2, steps)), dma((2, 2, steps)), dma((2, 2, steps)),
+        dma((2, 2, far, 2)), dma((2, 2, far, 2)), dma((2, 1 + 4 * far)), dma((2, 1 + 4 * far)),
+        dma((2 * nx,)), dma((1,)), dma((nz,)), dma((nz,)), dma((2, max(1, ny // 2))), dma((2, max(1, ny // 2))),
+        dma((nx,)), dma((nx,)),
+        dma((2, steps)), dma((2, steps)),
         dma((ny,)), dma((ny,)), dma((nz,)), dma((nz,)),
     ]
     return pl.pallas_call(

time: 77.5 us -> 83.9 us (1.083)
  the two profiles are of different devices: /device:TPU:2 before, /device:TPU:135 now
where the time goes in v3:
time: 83.9 us; the launch traced here: 83.8 us
  Pallas kernels  81.8 us (97%)
  local copies, waits for them, and re-layouts  1.31 us (2%)
    pallas_call x1, Pallas kernels, local(): pl.pallas_call(functools.partial(kernel, nx, ny, nz, cap), out_shape=(plt...  81.8 us

profile of v3, /device:TPU:135, one launch (start us, length us, event | category | flops | bytes accessed | tf_op | source)
XLA Modules:
  0.0 83.8 jit_solution(6350172404376055054)
XLA Ops:
  0.6 81.8 %shard_map.122 = (bf16[224,128]{1,0:T(8,128)(2,1)S(1)}, bf16[224,512]{1,0:T(8,128)(2,1)S(1)}) custom-call(s32[2,128]{1,0:T(2,128)} %bitcast.2, f32[2,128]{1,0:T(2,128)} %bitcast.3, bf16[1,152,384]{2,1,0:T(8,128)(2,1)} %back_h.1, bf16[1,152,384]{2,1,0:T(8,128)(2,1)} %sgate_h.1, bf16[1,152,384]{2,1,0:T(8,128)(2,1)} %sup_h.1, bf16[1,152,3584]{2,1,0:T(8,128)(2,1)} %egw_h.1, ...), custom_call_target="tpu_custom_call" | custom-call | tf_op jit(solution)/shard_map/pallas_call | solution.py:468
  82.5 0.6 copy.15
  83.1 0.7 copy.16

commit v4 on v2

--- a/solution.py
+++ b/solution.py
@@ -59,47 +59,6 @@
     for load in loads:
         load.start()
 
-    barrier = pltpu.get_barrier_semaphore()
-    y_z = [dict(expert=(y + k) % ny) for k in range(1, ny)]
-    y_z += [dict(tensor=(z + k) % nz) for k in range(1, nz)]
-
-    def signal(sem, **where):
-        pl.semaphore_signal(sem, inc=1, device_id=where, device_id_type=MESH)
-
-    @pl.when(c == 0)
-    def _():
-        signal(barrier, dp=dp_of(1))
-        signal(barrier, dp=dp_of(-1))
-        pl.semaphore_wait(barrier, 3)
-        signal(meet.at[0], dp=dp_of(1))
-        signal(meet.at[0], dp=dp_of(-1))
-        pl.semaphore_wait(meet.at[0], 2)
-        signal(meet.at[1], dp=sib)
-
-    @pl.when(c == 1)
-    def _():
-        signal(barrier, dp=sib)
-        pl.semaphore_wait(meet.at[1], 1)
-        for where in y_z:
-            signal(barrier, **where)
-
-    def meet_y_z():
-        @pl.when(c == 1)
-        def _():
-            if y_z:
-                pl.semaphore_wait(barrier, len(y_z))
-            signal(meet.at[2], dp=sib)
-
-        @pl.when(c == 0)
-        def _():
-            pl.semaphore_wait(meet.at[2], 1)
-
-    pending = []
-
-    def go(copy):
-        copy.start()
-        pending.append(copy)
-
     def x_part(dp, t, h, size):
         return x_all.at[rows(dp * feat + h * half, size), pl.ds(t * part, part)]
 
@@ -115,11 +74,12 @@
             src = inb_h.at[:, pl.ds(t * part, part)]
         return rdma(src, dst, sib_s.at[t, slot], sib_r.at[t, slot], dp=sib)
 
-    def ag_open(t):
-        for h in range(2):
-            for d in range(2):
-                go(ag_copy(d, t, 1, h, me))
-        go(sib_copy(t, 0, 0, me, feat))
+    def ag_open():
+        copies = []
+        for t in range(2):
+            copies += [ag_copy(d, t, 1, h, me) for h in range(2) for d in range(2)]
+            copies.append(sib_copy(t, 0, 0, me, feat))
+        return copies
 
     def ag_step(t, hop):
         for h in range(2):
@@ -141,8 +101,52 @@
                         origin = chip(-(1 - 2 * d) * hop) * 2 + 1 - c
                         sib_copy(t, 1 + (hop - 1) * 4 + d * 2 + h, h, origin, half).wait_recv()
 
-    for t in range(2):
-        ag_open(t)
+    barrier = pltpu.get_barrier_semaphore()
+    y_z = [dict(expert=(y + k) % ny) for k in range(1, ny)]
+    y_z += [dict(tensor=(z + k) % nz) for k in range(1, nz)]
+
+    def signal(sem, **where):
+        pl.semaphore_signal(sem, inc=1, device_id=where, device_id_type=MESH)
+
+    @pl.when(c == 0)
+    def _():
+        signal(barrier, dp=dp_of(1))
+        signal(barrier, dp=dp_of(-1))
+        pl.semaphore_wait(barrier, 3)
+        signal(meet.at[0], dp=dp_of(1))
+        signal(meet.at[0], dp=dp_of(-1))
+        for copy in ag_open():
+            copy.start()
+        pl.semaphore_wait(meet.at[0], 2)
+        signal(meet.at[1], dp=sib)
+
+    @pl.when(c == 1)
+    def _():
+        signal(barrier, dp=sib)
+        pl.semaphore_wait(meet.at[1], 1)
+        for copy in ag_open():
+            copy.start()
+        for where in y_z:
+            signal(barrier, **where)
+
+    def meet_y_z():
+        @pl.when(c == 1)
+        def _():
+            if y_z:
+                pl.semaphore_wait(barrier, len(y_z))
+            signal(meet.at[2], dp=sib)
+
+        @pl.when(c == 0)
+        def _():
+            pl.semaphore_wait(meet.at[2], 1)
+
+    pending = []
+
+    def go(copy):
+        copy.start()
+        pending.append(copy)
+
+    pending.extend(ag_open())
 
     for i in range(3):
         loads[i].wait()

time: 77.5 us -> 76.4 us (0.986)
  the two profiles are of different devices: /device:TPU:2 before, /device:TPU:4 now
where the time goes in v4:
time: 76.4 us; the launch traced here: 76.2 us
  Pallas kernels  74.3 us (97%)
  local copies, waits for them, and re-layouts  1.31 us (2%)
    pallas_call x1, Pallas kernels, local(): pl.pallas_call(functools.partial(kernel, nx, ny, nz, cap), out_shape=(plt...  74.3 us

profile of v4, /device:TPU:4, one launch (start us, length us, event | category | flops | bytes accessed | tf_op | source)
XLA Modules:
  0.0 76.2 jit_solution(7222851207381644461)
XLA Ops:
  0.6 74.3 %shard_map.122 = (bf16[224,128]{1,0:T(8,128)(2,1)S(1)}, bf16[224,512]{1,0:T(8,128)(2,1)S(1)}) custom-call(s32[2,128]{1,0:T(2,128)} %bitcast.2, f32[2,128]{1,0:T(2,128)} %bitcast.3, bf16[1,152,384]{2,1,0:T(8,128)(2,1)} %back_h.1, bf16[1,152,384]{2,1,0:T(8,128)(2,1)} %sgate_h.1, bf16[1,152,384]{2,1,0:T(8,128)(2,1)} %sup_h.1, bf16[1,152,3584]{2,1,0:T(8,128)(2,1)} %egw_h.1, ...), custom_call_target="tpu_custom_call" | custom-call | tf_op jit(solution)/shard_map/pallas_call | solution.py:403
  74.9 0.6 copy.15
  75.5 0.7 copy.16

commit v5 on v4

--- a/solution.py
+++ b/solution.py
@@ -344,18 +344,18 @@
     rs_step(dflow[1], 1, False)
     rs_step(dflow[0], 2, True)
     rs_step(dflow[0], 2, False)
+    rs_step(dflow[1], 2, True)
+    rs_step(dflow[1], 2, False)
+    dense_recv(0, 3)
+    dense_recv(1, 3)
+    rs_step(dflow[0], 3, True)
+    rs_step(dflow[0], 3, False)
     for k in range(1, ny):
         y_wait(k)
     a3[...] = jnp.dot(perm[...], a2[...], preferred_element_type=F32).astype(BF)
     for k in range(1, nz):
         go(z_copy(k))
     a4[rows(z * nz_rows, nz_rows), :] = a3[rows(z * nz_rows, nz_rows), :]
-    rs_step(dflow[1], 2, True)
-    rs_step(dflow[1], 2, False)
-    dense_recv(0, 3)
-    dense_recv(1, 3)
-    rs_step(dflow[0], 3, True)
-    rs_step(dflow[0], 3, False)
     rs_step(dflow[1], 3, True)
     rs_step(dflow[1], 3, False)
     for t in range(2):

time: 76.4 us -> 76.4 us (level)
  no operation moved by 1% of the time
where the time goes in v5:
time: 76.4 us; the launch traced here: 76.2 us
  Pallas kernels  74.3 us (97%)
  local copies, waits for them, and re-layouts  1.31 us (2%)
    pallas_call x1, Pallas kernels, local(): pl.pallas_call(functools.partial(kernel, nx, ny, nz, cap), out_shape=(plt...  74.3 us

profile of v5, /device:TPU:4, one launch (start us, length us, event | category | flops | bytes accessed | tf_op | source)
XLA Modules:
  0.0 76.2 jit_solution(13867060789833227471)
XLA Ops:
  0.6 74.3 %shard_map.122 = (bf16[224,128]{1,0:T(8,128)(2,1)S(1)}, bf16[224,512]{1,0:T(8,128)(2,1)S(1)}) custom-call(s32[2,128]{1,0:T(2,128)} %bitcast.2, f32[2,128]{1,0:T(2,128)} %bitcast.3, bf16[1,152,384]{2,1,0:T(8,128)(2,1)} %back_h.1, bf16[1,152,384]{2,1,0:T(8,128)(2,1)} %sgate_h.1, bf16[1,152,384]{2,1,0:T(8,128)(2,1)} %sup_h.1, bf16[1,152,3584]{2,1,0:T(8,128)(2,1)} %egw_h.1, ...), custom_call_target="tpu_custom_call" | custom-call | tf_op jit(solution)/shard_map/pallas_call | solution.py:403
  74.9 0.6 copy.15
  75.5 0.7 copy.16
